TPU v7x, 32 devices: a whole 2x2x4 slice. The times are simulated.
32 devices in a mesh: dp: 4 (over x, core), fsdp: 8 (over z, y).
Axes of the slice: x: 2, y: 2, z: 4, core: 2. Of those that a mesh axis runs over, the one named last changes fastest.
Arguments:
- latents: bfloat16 [128, 64, 1536], P(('dp', 'fsdp')), may hold values from -6 to 6
- media: bfloat16 [576, 48, 1536], P(('dp', 'fsdp')), may hold values from -6 to 6
- frame_counts: int32 [128], P(('dp', 'fsdp')), may hold values from 1 to 8, as said below
- cotangent: bfloat16 [128, 64, 1536], P(('dp', 'fsdp')), may hold values from -6 to 6
- w_qkv: float32 [1536, 3, 1536], P(('dp', 'fsdp')), may hold values from -0.15625 to 0.15625
- m_qkv: float32 [1536, 3, 1536], P(('dp', 'fsdp')), may hold values from -0.00012207031 to 0.00012207031
- v_qkv: float32 [1536, 3, 1536], P(('dp', 'fsdp')), may hold values from 3.532127e-11 to 1.4128508e-10
- w_out: float32 [1536, 1536], P(('dp', 'fsdp')), may hold values from -1.25 to 1.25
- m_out: float32 [1536, 1536], P(('dp', 'fsdp')), may hold values from -0.00012207031 to 0.00012207031
- v_out: float32 [1536, 1536], P(('dp', 'fsdp')), may hold values from 7.064254e-12 to 2.8257017e-11
- w_up: float32 [1536, 6144], P(('dp', 'fsdp')), may hold values from -0.15625 to 0.15625
- m_up: float32 [1536, 6144], P(('dp', 'fsdp')), may hold values from -0.00012207031 to 0.00012207031
- v_up: float32 [1536, 6144], P(('dp', 'fsdp')), may hold values from 3.532127e-11 to 1.4128508e-10
- w_down: float32 [6144, 1536], P(('dp', 'fsdp')), may hold values from -0.078125 to 0.078125
- m_down: float32 [6144, 1536], P(('dp', 'fsdp')), may hold values from -0.00012207031 to 0.00012207031
- v_down: float32 [6144, 1536], P(('dp', 'fsdp')), may hold values from 3.532127e-11 to 1.4128508e-10
- time_table: float32 [1536, 8], P(('dp', 'fsdp')), may hold values from -3 to 3
- m_time: float32 [1536, 8], P(('dp', 'fsdp')), may hold values from -0.00036621094 to 0.00036621094
- v_time: float32 [1536, 8], P(('dp', 'fsdp')), may hold values from 3.1789144e-10 to 1.2715657e-09
- gains: float32 [1536, 3], P(('dp', 'fsdp')), may hold values from 0.3 to 2.5, as said below
- m_gains: float32 [1536, 3], P(('dp', 'fsdp')), may hold values from -0.00036621094 to 0.00036621094
- v_gains: float32 [1536, 3], P(('dp', 'fsdp')), may hold values from 3.1789144e-10 to 1.2715657e-09
Outputs:
- new_latents: bfloat16 [128, 64, 1536], P(('dp', 'fsdp'))
- d_latents: float32 [128, 64, 1536], P(('dp', 'fsdp'))
- grad_norm: float32 [], replicated
- new_w_qkv: float32 [1536, 3, 1536], P(('dp', 'fsdp'))
- new_m_qkv: float32 [1536, 3, 1536], P(('dp', 'fsdp'))
- new_v_qkv: float32 [1536, 3, 1536], P(('dp', 'fsdp'))
- new_w_out: float32 [1536, 1536], P(('dp', 'fsdp'))
- new_m_out: float32 [1536, 1536], P(('dp', 'fsdp'))
- new_v_out: float32 [1536, 1536], P(('dp', 'fsdp'))
- new_w_up: float32 [1536, 6144], P(('dp', 'fsdp'))
- new_m_up: float32 [1536, 6144], P(('dp', 'fsdp'))
- new_v_up: float32 [1536, 6144], P(('dp', 'fsdp'))
- new_w_down: float32 [6144, 1536], P(('dp', 'fsdp'))
- new_m_down: float32 [6144, 1536], P(('dp', 'fsdp'))
- new_v_down: float32 [6144, 1536], P(('dp', 'fsdp'))
- new_time_table: float32 [1536, 8], P(('dp', 'fsdp'))
- new_m_time: float32 [1536, 8], P(('dp', 'fsdp'))
- new_v_time: float32 [1536, 8], P(('dp', 'fsdp'))
- new_gains: float32 [1536, 3], P(('dp', 'fsdp'))
- new_m_gains: float32 [1536, 3], P(('dp', 'fsdp'))
- new_v_gains: float32 [1536, 3], P(('dp', 'fsdp'))
Inputs may be any that keep to these rules, and one draw needn't show every extreme that they name: `frame_counts`: each item slot holds one image of 1 frame or one clip of 8 frames; the frames of one device's 4 slots never exceed 18, and on some device of every draw they fill all 18. Positive gains.
All inputs are finite; a program needn't handle non-finite values.
Results may differ from a plain program's by a relative error of at most 0.022.
Values may be sent and summed in bfloat16 or wider, within the bound.
A program may use at most 320 MiB of HBM per device.

v0:
```python
import jax
import jax.numpy as jnp
from jax import lax
from jax.sharding import PartitionSpec as P

HEADS = 16
STEP = 10
highest = lax.Precision.HIGHEST
norm_eps = 1e-05
clip_limit = 1.0
beta_one = 0.9
beta_two = 0.999
adam_eps = 1e-08
decay_rate = 0.1


def layer_norm(values_in, gain):
    mean_row = jnp.mean(values_in, axis=-1, keepdims=True)
    centered = values_in - mean_row
    var_row = jnp.mean(centered * centered, axis=-1, keepdims=True)
    return centered * lax.rsqrt(var_row + norm_eps) * gain


def exact_gelu(values_in):
    return jax.nn.gelu(values_in, approximate=False)


def frame_tables(counts, frame_slots, time_len):
    slot_total = counts.shape[0]
    slot_ends = jnp.cumsum(counts)
    slot_starts = slot_ends - counts
    frame_ids = jnp.arange(frame_slots, dtype=jnp.int32)
    frame_owner = jnp.sum((frame_ids[:, None] >= slot_ends[None, :]).astype(jnp.int32), axis=1)
    slot_ids = jnp.arange(slot_total, dtype=jnp.int32)
    start_of = jnp.sum(
        jnp.where(frame_owner[:, None] == slot_ids[None, :], slot_starts[None, :], 0), axis=1
    )
    time_index = frame_ids - start_of
    live_frame = frame_owner < slot_total
    time_ids = jnp.arange(time_len, dtype=jnp.int32)
    time_hot = ((time_index[:, None] == time_ids[None, :]) & live_frame[:, None]).astype(
        jnp.float32
    )
    return (frame_owner, time_hot)


def gather_params(part_qkv, part_out, part_up, part_down, part_time, part_gains):
    inner_part = (
        lax.all_gather(part_qkv, "fsdp", axis=0, tiled=True),
        lax.all_gather(part_out, "fsdp", axis=0, tiled=True),
        lax.all_gather(part_up, "fsdp", axis=0, tiled=True),
        lax.all_gather(part_down, "fsdp", axis=0, tiled=True),
        lax.all_gather(part_time, "fsdp", axis=0, tiled=True),
        lax.all_gather(part_gains, "fsdp", axis=0, tiled=True),
    )
    return (
        lax.all_gather(inner_part[0], "dp", axis=0, tiled=True),
        lax.all_gather(inner_part[1], "dp", axis=0, tiled=True),
        lax.all_gather(inner_part[2], "dp", axis=0, tiled=True),
        lax.all_gather(inner_part[3], "dp", axis=0, tiled=True),
        lax.all_gather(inner_part[4], "dp", axis=0, tiled=True),
        lax.all_gather(inner_part[5], "dp", axis=0, tiled=True),
    )


def reduce_grads(grad_qkv, grad_out, grad_up, grad_down, grad_time, grad_gains):
    outer_part = (
        lax.psum_scatter(
            grad_qkv.astype(jnp.bfloat16), "dp", scatter_dimension=0, tiled=True
        ).astype(jnp.float32),
        lax.psum_scatter(
            grad_out.astype(jnp.bfloat16), "dp", scatter_dimension=0, tiled=True
        ).astype(jnp.float32),
        lax.psum_scatter(
            grad_up.astype(jnp.bfloat16), "dp", scatter_dimension=0, tiled=True
        ).astype(jnp.float32),
        lax.psum_scatter(
            grad_down.astype(jnp.bfloat16), "dp", scatter_dimension=0, tiled=True
        ).astype(jnp.float32),
        lax.psum_scatter(
            grad_time.astype(jnp.bfloat16), "dp", scatter_dimension=0, tiled=True
        ).astype(jnp.float32),
        lax.psum_scatter(
            grad_gains.astype(jnp.bfloat16), "dp", scatter_dimension=0, tiled=True
        ).astype(jnp.float32),
    )
    return (
        lax.psum_scatter(
            outer_part[0].astype(jnp.bfloat16), "fsdp", scatter_dimension=0, tiled=True
        ).astype(jnp.float32),
        lax.psum_scatter(
            outer_part[1].astype(jnp.bfloat16), "fsdp", scatter_dimension=0, tiled=True
        ).astype(jnp.float32),
        lax.psum_scatter(
            outer_part[2].astype(jnp.bfloat16), "fsdp", scatter_dimension=0, tiled=True
        ).astype(jnp.float32),
        lax.psum_scatter(
            outer_part[3].astype(jnp.bfloat16), "fsdp", scatter_dimension=0, tiled=True
        ).astype(jnp.float32),
        lax.psum_scatter(
            outer_part[4].astype(jnp.bfloat16), "fsdp", scatter_dimension=0, tiled=True
        ).astype(jnp.float32),
        lax.psum_scatter(
            outer_part[5].astype(jnp.bfloat16), "fsdp", scatter_dimension=0, tiled=True
        ).astype(jnp.float32),
    )


def masked_scores(q_heads, k_heads, allowed, score_scale):
    scores = (
        jnp.einsum("qhe,khe->hqk", q_heads, k_heads, preferred_element_type=jnp.float32)
        * score_scale
    )
    return jnp.where(allowed[None, :, :], scores, -1e30)


def adamw_step(weight, first, second, grad, factor, rate):
    clipped = grad * factor
    first_new = beta_one * first + (1.0 - beta_one) * clipped
    second_new = beta_two * second + (1.0 - beta_two) * clipped * clipped
    first_hat = first_new / (1.0 - beta_one**STEP)
    second_hat = second_new / (1.0 - beta_two**STEP)
    weight_new = weight - rate * (
        first_hat / (jnp.sqrt(second_hat) + adam_eps) + decay_rate * weight
    )
    return (weight_new, first_new, second_new)


def on_device(
    latents,
    media,
    frame_counts,
    cotangent,
    w_qkv,
    m_qkv,
    v_qkv,
    w_out,
    m_out,
    v_out,
    w_up,
    m_up,
    v_up,
    w_down,
    m_down,
    v_down,
    time_table,
    m_time,
    v_time,
    gains,
    m_gains,
    v_gains,
):
    low_qkv = w_qkv.astype(jnp.bfloat16)
    low_out = w_out.astype(jnp.bfloat16)
    low_up = w_up.astype(jnp.bfloat16)
    low_down = w_down.astype(jnp.bfloat16)
    low_time = time_table.astype(jnp.bfloat16)
    low_gains = gains.astype(jnp.bfloat16)
    full_qkv, full_out, full_up, full_down, full_time, full_gains = gather_params(
        low_qkv, low_out, low_up, low_down, low_time, low_gains
    )
    item_slots, lat_count, model_width = latents.shape
    frame_slots, patch_rows, unused_width = media.shape
    queries_n = item_slots * lat_count
    media_rows = frame_slots * patch_rows
    head_size = model_width // HEADS
    score_scale = 1.0 / head_size**0.5
    frame_owner, time_hot = frame_tables(frame_counts, frame_slots, full_time.shape[1])
    time_f32 = full_time.astype(jnp.float32)
    gains_f32 = full_gains.astype(jnp.float32)
    frame_time = jnp.dot(time_hot, time_f32.T, precision=highest)
    mixed = media.astype(jnp.float32) + frame_time[:, None, :]
    media_norm, media_back = jax.vjp(layer_norm, mixed, gains_f32[:, 0])
    media_low = media_norm.astype(jnp.bfloat16).reshape(media_rows, model_width)
    lat_rows = latents.reshape(queries_n, model_width).astype(jnp.float32)
    lat_norm, lat_back = jax.vjp(layer_norm, lat_rows, gains_f32[:, 1])
    lat_low = lat_norm.astype(jnp.bfloat16)
    keys_in = jnp.concatenate([media_low, lat_low], axis=0)
    key_rows = keys_in.shape[0]
    qkv_flat = full_qkv.reshape(model_width, 3 * model_width)
    queries = jnp.dot(
        lat_low, qkv_flat[:, :model_width], preferred_element_type=jnp.float32
    ).astype(jnp.bfloat16)
    key_value = jnp.dot(
        keys_in, qkv_flat[:, model_width:], preferred_element_type=jnp.float32
    ).astype(jnp.bfloat16)
    q_heads = queries.reshape(queries_n, HEADS, head_size)
    k_heads = key_value[:, :model_width].reshape(key_rows, HEADS, head_size)
    v_heads = key_value[:, model_width:].reshape(key_rows, HEADS, head_size)
    query_owner = jnp.arange(queries_n, dtype=jnp.int32) // lat_count
    key_owner = jnp.concatenate([jnp.repeat(frame_owner, patch_rows), query_owner], axis=0)
    allowed = query_owner[:, None] == key_owner[None, :]
    scores = masked_scores(q_heads, k_heads, allowed, score_scale)
    row_top = jnp.max(scores, axis=-1, keepdims=True)
    row_total = jnp.sum(jnp.exp(scores - row_top), axis=-1, keepdims=True)
    log_total = row_top + jnp.log(row_total)
    probs_low = jnp.exp(scores - log_total).astype(jnp.bfloat16)
    attended = jnp.einsum("hqk,khe->qhe", probs_low, v_heads, preferred_element_type=jnp.float32)
    attended = attended.reshape(queries_n, model_width).astype(jnp.bfloat16)
    middle = lat_rows + jnp.dot(attended, full_out, preferred_element_type=jnp.float32)
    hidden, ffn_back = jax.vjp(layer_norm, middle, gains_f32[:, 2])
    hidden_low = hidden.astype(jnp.bfloat16)
    pre_act = jnp.dot(hidden_low, full_up, preferred_element_type=jnp.float32)
    activated, gelu_back = jax.vjp(exact_gelu, pre_act)
    act_low = activated.astype(jnp.bfloat16)
    result = middle + jnp.dot(act_low, full_down, preferred_element_type=jnp.float32)
    new_latents = result.astype(jnp.bfloat16).reshape(item_slots, lat_count, model_width)
    back_qkv, back_out, back_up, back_down, back_time, back_gains = gather_params(
        low_qkv, low_out, low_up, low_down, low_time, low_gains
    )
    d_result = cotangent.reshape(queries_n, model_width)
    g_down = jnp.einsum("qf,qd->fd", act_low, d_result, preferred_element_type=jnp.float32)
    d_act = jnp.einsum("qd,fd->qf", d_result, back_down, preferred_element_type=jnp.float32)
    d_pre = gelu_back(d_act)[0].astype(jnp.bfloat16)
    g_up = jnp.einsum("qd,qf->df", hidden_low, d_pre, preferred_element_type=jnp.float32)
    d_hidden = jnp.einsum("qf,df->qd", d_pre, back_up, preferred_element_type=jnp.float32)
    d_middle_ln, g_gain_ffn = ffn_back(d_hidden)
    d_middle = d_result.astype(jnp.float32) + d_middle_ln
    d_branch = d_middle.astype(jnp.bfloat16)
    g_out = jnp.einsum("qe,qd->ed", attended, d_branch, preferred_element_type=jnp.float32)
    d_attended = jnp.einsum(
        "qd,ed->qe", d_branch, back_out, preferred_element_type=jnp.float32
    ).astype(jnp.bfloat16)
    scores_again = masked_scores(q_heads, k_heads, allowed, score_scale)
    probs = jnp.exp(scores_again - log_total)
    probs_again = probs.astype(jnp.bfloat16)
    d_att_heads = d_attended.reshape(queries_n, HEADS, head_size)
    d_probs = jnp.einsum("qhe,khe->hqk", d_att_heads, v_heads, preferred_element_type=jnp.float32)
    row_dot = jnp.sum(probs * d_probs, axis=-1, keepdims=True)
    d_scores = (probs * (d_probs - row_dot)).astype(jnp.bfloat16)
    d_queries = (
        (
            jnp.einsum("hqk,khe->qhe", d_scores, k_heads, preferred_element_type=jnp.float32)
            * score_scale
        )
        .reshape(queries_n, model_width)
        .astype(jnp.bfloat16)
    )
    d_keys = (
        (
            jnp.einsum("hqk,qhe->khe", d_scores, q_heads, preferred_element_type=jnp.float32)
            * score_scale
        )
        .reshape(key_rows, model_width)
        .astype(jnp.bfloat16)
    )
    d_values = (
        jnp.einsum("hqk,qhe->khe", probs_again, d_att_heads, preferred_element_type=jnp.float32)
        .reshape(key_rows, model_width)
        .astype(jnp.bfloat16)
    )
    g_query = jnp.einsum("qd,qe->de", lat_low, d_queries, preferred_element_type=jnp.float32)
    d_key_value = jnp.concatenate([d_keys, d_values], axis=1)
    g_key_value = jnp.einsum("kd,kx->dx", keys_in, d_key_value, preferred_element_type=jnp.float32)
    g_qkv = jnp.concatenate([g_query, g_key_value], axis=1).reshape(model_width, 3, model_width)
    back_flat = back_qkv.reshape(model_width, 3 * model_width)
    d_keys_in = jnp.einsum(
        "kx,dx->kd", d_key_value, back_flat[:, model_width:], preferred_element_type=jnp.float32
    )
    d_lat_norm = (
        jnp.einsum(
            "qe,de->qd", d_queries, back_flat[:, :model_width], preferred_element_type=jnp.float32
        )
        + d_keys_in[media_rows:]
    )
    d_lat_ln, g_gain_lat = lat_back(d_lat_norm)
    d_latents = (d_middle + d_lat_ln).reshape(item_slots, lat_count, model_width)
    d_mixed, g_gain_media = media_back(
        d_keys_in[:media_rows].reshape(frame_slots, patch_rows, model_width)
    )
    frame_grad = jnp.sum(d_mixed, axis=1)
    g_time = jnp.einsum("fd,ft->dt", frame_grad, time_hot, precision=highest)
    g_gains = jnp.stack([g_gain_media, g_gain_lat, g_gain_ffn], axis=1)
    reduced = reduce_grads(g_qkv, g_out, g_up, g_down, g_time, g_gains)
    local_sq = jnp.zeros((), jnp.float32)
    for grad in reduced:
        local_sq = local_sq + jnp.sum(grad * grad)
    grad_norm = jnp.sqrt(lax.psum(local_sq, ("dp", "fsdp")))
    factor = jnp.minimum(1.0, clip_limit / (grad_norm + 1e-06))
    masters = (w_qkv, w_out, w_up, w_down, time_table, gains)
    firsts = (m_qkv, m_out, m_up, m_down, m_time, m_gains)
    seconds = (v_qkv, v_out, v_up, v_down, v_time, v_gains)
    rates = (0.02, 0.1, 0.02, 0.01, 0.2, 0.5)
    updated = []
    for index in range(6):
        updated.extend(
            adamw_step(
                masters[index], firsts[index], seconds[index], reduced[index], factor, rates[index]
            )
        )
    return (
        new_latents,
        d_latents,
        grad_norm,
        updated[0],
        updated[1],
        updated[2],
        updated[3],
        updated[4],
        updated[5],
        updated[6],
        updated[7],
        updated[8],
        updated[9],
        updated[10],
        updated[11],
        updated[12],
        updated[13],
        updated[14],
        updated[15],
        updated[16],
        updated[17],
    )


def solution(mesh):
    placed = (
        P(("dp", "fsdp"), None, None),
        P(("dp", "fsdp"), None, None),
        P(("dp", "fsdp")),
        P(("dp", "fsdp"), None, None),
        P(("dp", "fsdp"), None, None),
        P(("dp", "fsdp"), None, None),
        P(("dp", "fsdp"), None, None),
        P(("dp", "fsdp"), None),
        P(("dp", "fsdp"), None),
        P(("dp", "fsdp"), None),
        P(("dp", "fsdp"), None),
        P(("dp", "fsdp"), None),
        P(("dp", "fsdp"), None),
        P(("dp", "fsdp"), None),
        P(("dp", "fsdp"), None),
        P(("dp", "fsdp"), None),
        P(("dp", "fsdp"), None),
        P(("dp", "fsdp"), None),
        P(("dp", "fsdp"), None),
        P(("dp", "fsdp"), None),
        P(("dp", "fsdp"), None),
        P(("dp", "fsdp"), None),
    )
    return jax.shard_map(
        on_device,
        mesh=mesh,
        in_specs=placed,
        out_specs=(
            P(("dp", "fsdp"), None, None),
            P(("dp", "fsdp"), None, None),
            P(),
            P(("dp", "fsdp"), None, None),
            P(("dp", "fsdp"), None, None),
            P(("dp", "fsdp"), None, None),
            P(("dp", "fsdp"), None),
            P(("dp", "fsdp"), None),
            P(("dp", "fsdp"), None),
            P(("dp", "fsdp"), None),
            P(("dp", "fsdp"), None),
            P(("dp", "fsdp"), None),
            P(("dp", "fsdp"), None),
            P(("dp", "fsdp"), None),
            P(("dp", "fsdp"), None),
            P(("dp", "fsdp"), None),
            P(("dp", "fsdp"), None),
            P(("dp", "fsdp"), None),
            P(("dp", "fsdp"), None),
            P(("dp", "fsdp"), None),
            P(("dp", "fsdp"), None),
        ),
        check_vma=False,
    )
```

profile of v0, /device:TPU:0, one launch (start us, length us, event | category | flops | bytes accessed | tf_op | source)
XLA Modules:
  0.0 1890.9 jit_solution(5706644227998352457)
XLA Ops:
  7.2 2.1 convert_element_type.180
  11.1 2.1 convert_element_type.189
  14.3 64.4 %all-gather.11.cloned.1.call-done = bf16[384,3,1536]{2,0,1:T(8,128)(2,1)} async-done(((bf16[48,3,1536]{2,0,1:T(8,128)(2,1)}), bf16[384,3,1536]{2,0,1:T(8,128)(2,1)}) %all-gather.11.cloned.1.call-update) | async-done | bytes 3538960 | tf_op jit(solution)/shard_map/all_gather | solution.py:49
  78.7 6.0 copy.105
  84.8 36.2 %all-gather.15.cloned.1.call-done = bf16[384,1536]{1,0:T(8,128)(2,1)} async-done(((bf16[48,1536]{1,0:T(8,128)(2,1)}), bf16[384,1536]{1,0:T(8,128)(2,1)}) %all-gather.15.cloned.1.call-update) | async-done | bytes 1179664 | tf_op jit(solution)/shard_map/all_gather | solution.py:50
  121.1 81.4 %all-gather.19.cloned.1.call-done = bf16[384,6144]{1,0:T(8,128)(2,1)} async-done(((bf16[48,6144]{1,0:T(8,128)(2,1)}), bf16[384,6144]{1,0:T(8,128)(2,1)}) %all-gather.19.cloned.1.call-update) | async-done | bytes 4718608 | tf_op jit(solution)/shard_map/all_gather | solution.py:51
  202.6 80.6 %all-gather.23.cloned.1.call-done = bf16[1536,1536]{1,0:T(8,128)(2,1)} async-done(((bf16[192,1536]{1,0:T(8,128)(2,1)}), bf16[1536,1536]{1,0:T(8,128)(2,1)}) %all-gather.23.cloned.1.call-update) | async-done | bytes 4718608 | tf_op jit(solution)/shard_map/all_gather | solution.py:52
  285.1 17.7 all-gather.1
  303.4 5.2 all_gather.47
  308.6 26.0 %all-gather = bf16[8,48,8]{1,2,0:T(8,128)(2,1)S(1)} all-gather(bf16[1,48,8]{1,2,0:T(8,128)(2,1)S(1)} %convert_bitcast_fusion), channel_id=1, replica_groups=mesh['dp'=4,'fsdp'=8] {'fsdp'}, dimensions={0}, use_global_device_ids=true | all-gather | bytes 6912 | tf_op jit(solution)/shard_map/all_gather | solution.py:53
  334.7 5.5 all_gather.45
  345.3 2.5 multiply_convert_fusion.3
  347.8 26.0 %all-gather.13.cloned.1.call-done = bf16[1536,3,1536]{0,2,1:T(8,128)(2,1)} async-done(((bf16[384,3,1536]{0,2,1:T(8,128)(2,1)}), bf16[1536,3,1536]{0,2,1:T(8,128)(2,1)}) %all-gather.13.cloned.1.call-update) | async-done | bytes 14155792 | tf_op jit(solution)/shard_map/all_gather | solution.py:57
  373.8 4.8 fusion.22
  378.6 2.3 copy.107
  380.8 14.0 convolution_convert_fusion.3
  394.8 3.4 fusion.87
  398.2 4.3 copy.108
  402.5 6.0 copy.106
  408.6 10.7 fusion.88
  419.9 12.1 exponential_reduce_fusion
  432.7 11.6 fusion.31
  444.4 4.4 fusion.89
  451.4 82.9 %all-gather.21.cloned.1.call-done = bf16[1536,6144]{1,0:T(8,128)(2,1)} async-done(((bf16[384,6144]{1,0:T(8,128)(2,1)}), bf16[1536,6144]{1,0:T(8,128)(2,1)}) %all-gather.21.cloned.1.call-update) | async-done | bytes 18874384 | tf_op jit(solution)/shard_map/all_gather | solution.py:59
  534.3 11.4 fusion.72
  545.7 110.2 %all-gather.25.cloned.1.call-done = bf16[6144,1536]{1,0:T(8,128)(2,1)} async-done(((bf16[1536,1536]{1,0:T(8,128)(2,1)}), bf16[6144,1536]{1,0:T(8,128)(2,1)}) %all-gather.25.cloned.1.call-update) | async-done | bytes 18874384 | tf_op jit(solution)/shard_map/all_gather | solution.py:60
  655.9 23.4 %add_convert_fusion = (bf16[256,6144]{1,0:T(8,128)(2,1)}, f32[256,6144]{1,0:T(8,128)}) fusion(f32[256,6144]{1,0:T(8,128)} %fusion.72, bf16[256,1536]{1,0:T(8,128)(2,1)} %bitcast.108, bf16[6144,1536]{1,0:T(8,128)(2,1)} %all-gather.25.cloned.1.call-done), kind=kOutput, calls=%fused_computation.22 | convolution fusion | flops 4945084416 | bytes 35389440 | tf_op jit(solution)/shard_map/qd,fd->qf/dot_general | solution.py:213
  679.4 11.8 multiply_reduce_fusion.4
  695.5 2.3 convolution_convert_fusion.7
  697.8 2.3 copy.109
  700.1 11.2 convolution_convert_fusion.6
  711.4 13.3 multiply_reduce_fusion
  724.7 12.7 multiply_convert_fusion
  739.2 4.6 multiply_convert_fusion.1
  743.8 15.7 fusion.2
  760.7 4.1 multiply_reduce_fusion.6
  767.0 2.0 fusion.28
  769.1 3.0 multiply_reduce_fusion.1
  774.7 3.6 convolution_convert_fusion.5
  779.4 3.6 convolution_convert_fusion.4
  783.0 6.8 copy.110
  789.8 18.2 convolution_convert_fusion.2
  808.0 12.5 pad_maximum_fusion
  821.9 12.3 convolution_convert_fusion.1
  834.5 5.7 multiply_convert_fusion.2
  841.9 9.1 convolution_convert_fusion
  852.3 16.1 reduce-scatter.22.cloned.1.call-done
  868.4 112.1 %reduce-scatter.34.cloned.1.call-done = bf16[384,4608]{1,0:T(8,128)(2,1)} async-done(((bf16[1536,4608]{1,0:T(8,128)(2,1)}), bf16[384,4608]{1,0:T(8,128)(2,1)}) %reduce-scatter.34.cloned.1.call-update) | async-done | bytes 3538960
  980.5 5.7 copy.125
  986.3 9.0 copy.112
  995.3 127.4 %reduce-scatter.26.cloned.1.call-done = bf16[384,6144]{1,0:T(8,128)(2,1)} async-done(((bf16[1536,6144]{1,0:T(8,128)(2,1)}), bf16[384,6144]{1,0:T(8,128)(2,1)}) %reduce-scatter.26.cloned.1.call-update) | async-done | bytes 4718608 | tf_op jit(solution)/shard_map/reduce_scatter | solution.py:74
  1122.9 141.9 %reduce-scatter.30.cloned.1.call-done = bf16[1536,1536]{1,0:T(8,128)(2,1)} async-done(((bf16[6144,1536]{1,0:T(8,128)(2,1)}), bf16[1536,1536]{1,0:T(8,128)(2,1)}) %reduce-scatter.30.cloned.1.call-update) | async-done | bytes 4718608 | tf_op jit(solution)/shard_map/reduce_scatter | solution.py:77
  1266.0 10.6 fusion.21
  1276.7 49.2 %reduce-scatter.42.cloned.1.call-done = bf16[48,3]{1,0:T(8,128)(2,1)} async-done(((bf16[384,3]{1,0:T(8,128)(2,1)}), bf16[48,3]{1,0:T(8,128)(2,1)}) %reduce-scatter.42.cloned.1.call-update) | async-done | bytes 304
  1327.3 58.7 %reduce-scatter.38.cloned.1.call-done = bf16[48,8]{1,0:T(8,128)(2,1)} async-done(((bf16[384,8]{1,0:T(8,128)(2,1)}), bf16[48,8]{1,0:T(8,128)(2,1)}) %reduce-scatter.38.cloned.1.call-update) | async-done | bytes 784
  1387.4 65.3 %reduce-scatter.24.cloned.1.call-done = bf16[48,1536]{1,0:T(8,128)(2,1)} async-done(((bf16[384,1536]{1,0:T(8,128)(2,1)}), bf16[48,1536]{1,0:T(8,128)(2,1)}) %reduce-scatter.24.cloned.1.call-update) | async-done | bytes 147472 | tf_op jit(solution)/shard_map/reduce_scatter | solution.py:91
  1454.3 171.0 %all-reduce.3.cloned.1.call-done = bf16[384,3,1536]{2,1,0:T(4,128)(2,1)} async-done(((bf16[384,3,1536]{2,1,0:T(4,128)(2,1)}), bf16[384,3,1536]{2,1,0:T(4,128)(2,1)}) %all-reduce.3.cloned.1.call-update) | async-done | bytes 3538960
  1628.7 95.0 %reduce-scatter.28.cloned.1.call-done = bf16[48,6144]{1,0:T(8,128)(2,1)} async-done(((bf16[384,6144]{1,0:T(8,128)(2,1)}), bf16[48,6144]{1,0:T(8,128)(2,1)}) %reduce-scatter.28.cloned.1.call-update) | async-done | bytes 589840 | tf_op jit(solution)/shard_map/reduce_scatter | solution.py:94
  1726.3 96.4 %reduce-scatter.32.cloned.1.call-done = bf16[192,1536]{1,0:T(8,128)(2,1)} async-done(((bf16[1536,1536]{1,0:T(8,128)(2,1)}), bf16[192,1536]{1,0:T(8,128)(2,1)}) %reduce-scatter.32.cloned.1.call-update) | async-done | bytes 589840 | tf_op jit(solution)/shard_map/reduce_scatter | solution.py:97
  1826.6 3.8 add_add_fusion.3
  1830.4 40.5 %psum.7 = f32[]{:T(128)} all-reduce(f32[]{:T(128)S(6)} %add.224), channel_id=1, replica_groups=mesh['dp'=4,'fsdp'=8] {'dp','fsdp'}, use_global_device_ids=true, to_apply=%region_40.41 | all-reduce | flops 1 | bytes 8 | tf_op jit(solution)/shard_map/psum | solution.py:278
  1872.9 3.7 multiply_subtract_fusion.2
  1877.8 2.4 multiply_subtract_fusion
  1880.2 2.4 multiply_subtract_fusion.1
  (287 shorter events, 45.5 us)
Async XLA Ops:
  7.2 6.1 copy-start.19
  7.2 71.5 %all-gather.11.cloned.1.call-start = ((), (), s32[]{:S(2)}) async-start(), calls=%async_computation.11 | async-start | bytes 3981312 | tf_op jit(solution)/shard_map/all_gather | solution.py:49
  9.3 111.7 %all-gather.15.cloned.1.call-start = ((), (), s32[]{:S(2)}) async-start(), calls=%async_computation.13 | async-start | bytes 1327104 | tf_op jit(solution)/shard_map/all_gather | solution.py:50
  11.1 191.4 %all-gather.19.cloned.1.call-start = ((), (), s32[]{:S(2)}) async-start(), calls=%async_computation.15 | async-start | bytes 5308416 | tf_op jit(solution)/shard_map/all_gather | solution.py:51
  13.3 269.9 %all-gather.23.cloned.1.call-start = ((), (), s32[]{:S(2)}) async-start(), calls=%async_computation.17 | async-start | bytes 5308416 | tf_op jit(solution)/shard_map/all_gather | solution.py:52
  14.2 359.5 %all-gather.13.cloned.1.call-start = ((), (), s32[]{:S(2)}) async-start(), calls=%async_computation.12 | async-start | bytes 17694720 | tf_op jit(solution)/shard_map/all_gather | solution.py:57
  84.8 359.6 %all-gather.17.cloned.1.call-start = ((), (), s32[]{:S(2)}) async-start(), calls=%async_computation.14 | async-start | bytes 5898240 | tf_op jit(solution)/shard_map/all_gather | solution.py:58
  121.1 413.2 %all-gather.21.cloned.1.call-start = ((), (), s32[]{:S(2)}) async-start(), calls=%async_computation.16 | async-start | bytes 23592960 | tf_op jit(solution)/shard_map/all_gather | solution.py:59
  202.5 80.7 %copy-start.2 = (bf16[4,64,1536]{2,1,0:T(8,128)(2,1)S(1)}, bf16[4,64,1536]{2,1,0:T(8,128)(2,1)}, u32[]{:S(2)}) copy-start(bf16[4,64,1536]{2,1,0:T(8,128)(2,1)} %param.22) | copy-start | bytes 2359300
  202.5 82.1 %copy-start.71 = (f32[48,3]{0,1:T(4,128)S(1)}, f32[48,3]{0,1:T(4,128)}, u32[]{:S(2)}) copy-start(f32[48,3]{0,1:T(4,128)} %param.41) | copy-start | bytes 1732
  202.5 100.4 %copy-start.82 = (s32[4]{0:T(128)S(1)}, s32[4]{0:T(128)}, u32[]{:S(2)}) copy-start(s32[4]{0:T(128)} %param.24) | copy-start | bytes 52
  202.5 106.1 %copy-start.62 = (f32[48,8]{0,1:T(8,128)S(1)}, f32[48,8]{0,1:T(8,128)}, u32[]{:S(2)}) copy-start(f32[48,8]{0,1:T(8,128)} %param.38) | copy-start | bytes 4612
  202.5 139.0 %copy-start = (bf16[18,48,1536]{2,1,0:T(8,128)(2,1)S(1)}, bf16[18,48,1536]{2,1,0:T(8,128)(2,1)}, u32[]{:S(2)}) copy-start(bf16[18,48,1536]{2,1,0:T(8,128)(2,1)} %param.23) | copy-start | bytes 7962628
  202.5 453.4 %all-gather.25.cloned.1.call-start = ((), (), s32[]{:S(2)}) async-start(), calls=%async_computation.18 | async-start | bytes 23592960 | tf_op jit(solution)/shard_map/all_gather | solution.py:60
  283.2 567.9 %reduce-scatter.40.cloned.1.call-start = ((), (), s32[]{:S(2)}) async-start(), calls=%async_computation.28 | async-start | bytes 491520
  283.4 19.7 %copy-start.54 = (f32[4,64]{1,0:T(4,128)}, f32[4,64]{1,0:T(4,128)S(1)}, u32[]{:S(2)}) copy-start(f32[4,64]{1,0:T(4,128)S(1)} %broadcast_multiply_fusion.1) | copy-start | bytes 3076
  283.5 64.3 %copy-start.58 = (f32[256]{0:T(256)}, f32[256]{0:T(256)S(1)}, u32[]{:S(2)}) copy-start(f32[256]{0:T(256)S(1)} %div.162) | copy-start | bytes 3076
  284.6 63.2 %copy-start.60 = (f32[256]{0:T(256)}, f32[256]{0:T(256)S(1)}, u32[]{:S(2)}) copy-start(f32[256]{0:T(256)S(1)} %rsqrt.34) | copy-start | bytes 3076
  345.3 28.5 %copy-start.34 = (bf16[256,1536]{1,0:T(8,128)(2,1)S(1)}, bf16[256,1536]{1,0:T(8,128)(2,1)}, u32[]{:S(2)}) copy-start(bf16[256,1536]{1,0:T(8,128)(2,1)} %multiply_convert_fusion.7) | copy-start | bytes 2359300
  373.8 7.1 copy-start.25
  655.9 23.4 %copy-start.5 = (f32[256,1536]{1,0:T(8,128)S(1)}, f32[256,1536]{1,0:T(8,128)}, u32[]{:S(2)}) copy-start(f32[256,1536]{1,0:T(8,128)} %copy-done.4) | copy-start | bytes 4718596
  655.9 23.4 %copy-start.42 = (f32[1536]{0:T(1024)S(1)}, f32[1536]{0:T(1024)}, u32[]{:S(2)}) copy-start(f32[1536]{0:T(1024)} %get-tuple-element.90) | copy-start | bytes 18436
  655.9 23.4 %copy-start.52 = (f32[256]{0:T(256)S(1)}, f32[256]{0:T(256)}, u32[]{:S(2)}) copy-start(f32[256]{0:T(256)} %copy-done.51) | copy-start | bytes 3076
  655.9 23.4 %copy-start.56 = (f32[256]{0:T(256)S(1)}, f32[256]{0:T(256)}, u32[]{:S(2)}) copy-start(f32[256]{0:T(256)} %fusion.66) | copy-start | bytes 3076
  679.3 16.2 slice-start
  679.3 11.8 copy-start.67
  679.3 16.2 slice-start.1
  700.1 11.2 copy-start.16
  739.1 20.8 %copy-start.10 = (bf16[16,96,256]{2,1,0:T(8,128)(2,1)}, bf16[16,96,256]{2,1,0:T(8,128)(2,1)S(1)}, u32[]{:S(2)}) copy-start(bf16[16,96,256]{2,1,0:T(8,128)(2,1)S(1)} %multiply_convert_fusion.5) | copy-start | bytes 2359300
  760.7 5.0 copy-start.1
  760.7 5.0 copy-start.13
  760.7 5.0 copy-start.37
  760.7 5.0 copy-start.45
  769.1 5.6 copy-start.8
  769.1 5.7 copy-start.24
  773.1 78.5 %reduce-scatter.36.cloned.1.call-start = ((), (), s32[]{:S(2)}) async-start(), calls=%async_computation.26 | async-start | bytes 491520
  774.7 93.7 %reduce-scatter.22.cloned.1.call-start = ((), (), s32[]{:S(2)}) async-start(), calls=%async_computation.19 | async-start | bytes 5898240 | tf_op jit(solution)/shard_map/reduce_scatter | solution.py:71
  778.3 202.2 %reduce-scatter.34.cloned.1.call-start = ((), (), s32[]{:S(2)}) async-start(), calls=%async_computation.25 | async-start | bytes 17694720
  783.0 6.8 copy-start.26
  820.6 302.2 %reduce-scatter.26.cloned.1.call-start = ((), (), s32[]{:S(2)}) async-start(), calls=%async_computation.21 | async-start | bytes 23592960 | tf_op jit(solution)/shard_map/reduce_scatter | solution.py:74
  834.2 430.5 %reduce-scatter.30.cloned.1.call-start = ((), (), s32[]{:S(2)}) async-start(), calls=%async_computation.23 | async-start | bytes 23592960 | tf_op jit(solution)/shard_map/reduce_scatter | solution.py:77
  834.5 7.4 copy-start.15
  851.0 474.8 %reduce-scatter.42.cloned.1.call-start = ((), (), s32[]{:S(2)}) async-start(), calls=%async_computation.29 | async-start | bytes 110592
  851.6 534.4 %reduce-scatter.38.cloned.1.call-start = ((), (), s32[]{:S(2)}) async-start(), calls=%async_computation.27 | async-start | bytes 110592
  852.2 600.5 %reduce-scatter.24.cloned.1.call-start = ((), (), s32[]{:S(2)}) async-start(), calls=%async_computation.20 | async-start | bytes 1327104 | tf_op jit(solution)/shard_map/reduce_scatter | solution.py:91
  868.4 756.9 %all-reduce.3.cloned.1.call-start = ((), (), s32[]{:S(2)}) async-start(), calls=%async_computation.30 | async-start | bytes 9437184
  995.3 728.4 %reduce-scatter.28.cloned.1.call-start = ((), (), s32[]{:S(2)}) async-start(), calls=%async_computation.22 | async-start | bytes 5308416 | tf_op jit(solution)/shard_map/reduce_scatter | solution.py:94
  1122.8 142.0 %copy-start.83 = (u32[32]{0:T(128)S(1)}, u32[32]{0:T(128)}, u32[]{:S(2)}) copy-start(u32[32]{0:T(128)} %constant.211) | copy-start | bytes 388
  1122.8 699.8 %reduce-scatter.32.cloned.1.call-start = ((), (), s32[]{:S(2)}) async-start(), calls=%async_computation.24 | async-start | bytes 5308416 | tf_op jit(solution)/shard_map/reduce_scatter | solution.py:97
  1266.0 560.5 %copy-start.65 = (f32[256]{0:T(256)S(1)}, f32[256]{0:T(256)}, u32[]{:S(2)}) copy-start(f32[256]{0:T(256)} %copy-done.64) | copy-start | bytes 3076
  1327.3 544.3 %copy-start.72 = (f32[48,3]{0,1:T(4,128)S(1)}, f32[48,3]{0,1:T(4,128)}, u32[]{:S(2)}) copy-start(f32[48,3]{0,1:T(4,128)} %param.41) | copy-start | bytes 1732
  1327.3 544.3 %copy-start.76 = (f32[48,3]{0,1:T(4,128)S(1)}, f32[48,3]{0,1:T(4,128)}, u32[]{:S(2)}) copy-start(f32[48,3]{0,1:T(4,128)} %param.42) | copy-start | bytes 1732
  1327.3 544.3 %copy-start.77 = (f32[48,3]{0,1:T(4,128)S(1)}, f32[48,3]{0,1:T(4,128)}, u32[]{:S(2)}) copy-start(f32[48,3]{0,1:T(4,128)} %param.43) | copy-start | bytes 1732
  1387.4 484.8 %copy-start.63 = (f32[48,8]{0,1:T(8,128)S(1)}, f32[48,8]{0,1:T(8,128)}, u32[]{:S(2)}) copy-start(f32[48,8]{0,1:T(8,128)} %param.38) | copy-start | bytes 4612
  1387.4 484.8 %copy-start.74 = (f32[48,8]{0,1:T(8,128)S(1)}, f32[48,8]{0,1:T(8,128)}, u32[]{:S(2)}) copy-start(f32[48,8]{0,1:T(8,128)} %param.39) | copy-start | bytes 4612
  1387.4 484.9 %copy-start.75 = (f32[48,8]{0,1:T(8,128)S(1)}, f32[48,8]{0,1:T(8,128)}, u32[]{:S(2)}) copy-start(f32[48,8]{0,1:T(8,128)} %param.40) | copy-start | bytes 4612
  1826.6 50.1 %copy-start.29 = (f32[48,1536]{1,0:T(8,128)S(1)}, f32[48,1536]{1,0:T(8,128)}, u32[]{:S(2)}) copy-start(f32[48,1536]{1,0:T(8,128)} %param.29) | copy-start | bytes 884740
  1830.3 46.3 %copy-start.35 = (bf16[48,1536]{1,0:T(8,128)(2,1)S(1)}, bf16[48,1536]{1,0:T(8,128)(2,1)}, u32[]{:S(2)}) copy-start(bf16[48,1536]{1,0:T(8,128)(2,1)} %reduce-scatter.24.cloned.1.call-done) | copy-start | bytes 442372
  1830.3 46.3 %copy-start.38 = (f32[48,1536]{1,0:T(8,128)S(1)}, f32[48,1536]{1,0:T(8,128)}, u32[]{:S(2)}) copy-start(f32[48,1536]{1,0:T(8,128)} %param.30) | copy-start | bytes 884740
  1830.3 46.3 %copy-start.39 = (f32[48,1536]{1,0:T(8,128)S(1)}, f32[48,1536]{1,0:T(8,128)}, u32[]{:S(2)}) copy-start(f32[48,1536]{1,0:T(8,128)} %param.31) | copy-start | bytes 884740
  1830.3 47.4 %copy-start.20 = (f32[192,1536]{1,0:T(8,128)S(1)}, f32[192,1536]{1,0:T(8,128)}, u32[]{:S(2)}) copy-start(f32[192,1536]{1,0:T(8,128)} %param.35) | copy-start | bytes 3538948
  1830.4 47.4 %copy-start.28 = (bf16[192,1536]{1,0:T(8,128)(2,1)S(1)}, bf16[192,1536]{1,0:T(8,128)(2,1)}, u32[]{:S(2)}) copy-start(bf16[192,1536]{1,0:T(8,128)(2,1)} %reduce-scatter.32.cloned.1.call-done) | copy-start | bytes 1769476
  1871.6 6.1 copy-start.30
  1871.6 6.1 copy-start.31
  (42 other events, 99.8 us)
Sparse Core Ops, SparseCore 0:
  10.8 67.8 all-gather.10
  81.5 39.5 all-gather.14
  123.8 78.6 all-gather.18
  205.1 78.0 all-gather.22
  284.6 89.1 all-gather.12
  375.2 37.4 all-gather.16
  414.3 120.0 all-gather.20
  535.9 120.0 all-gather.24
  773.3 20.8 reduce-scatter.39
  797.1 20.8 reduce-scatter.35
  820.5 47.8 reduce-scatter.21
  871.0 109.4 reduce-scatter.33
  983.3 139.4 reduce-scatter.25
  1125.2 139.4 reduce-scatter.29
  1268.2 57.6 reduce-scatter.41
  1329.3 56.6 reduce-scatter.37
  1389.6 63.0 reduce-scatter.23
  1456.6 168.6 all-reduce.2
  1629.4 94.2 reduce-scatter.27
  1727.6 95.0 reduce-scatter.31
where the time goes:
time: 1900 us; the launch traced here: 1890 us
  waiting for transfers between devices  1420 us (75%)
  matrix products  203 us (11%)
  blocking collectives  94.9 us (5%)
  other arithmetic  91.2 us (5%)
  local copies, waits for them, and re-layouts  62.6 us (3%)
  between operations  22 us (1%)
    unnamed x26, waiting for transfers between devices  392 us
    reduce_scatter x1, waiting for transfers between devices, reduce_grads(): lax.psum_scatter(grad_down.astype(jnp.bfloat16), 'dp', scatter_dimension=...  142 us
    reduce_scatter x1, waiting for transfers between devices, reduce_grads(): lax.psum_scatter(grad_up.astype(jnp.bfloat16), 'dp', scatter_dimension=0,...  127 us
    all_gather x1, waiting for transfers between devices, gather_params(): lax.all_gather(inner_part[3], 'dp', axis=0, tiled=True)  110 us
    reduce_scatter x1, waiting for transfers between devices, reduce_grads(): lax.psum_scatter(outer_part[3].astype(jnp.bfloat16), 'fsdp', scatter_dime...  96.4 us
    reduce_scatter x1, waiting for transfers between devices, reduce_grads(): lax.psum_scatter(outer_part[2].astype(jnp.bfloat16), 'fsdp', scatter_dime...  95 us
    all_gather x1, waiting for transfers between devices, gather_params(): lax.all_gather(inner_part[2], 'dp', axis=0, tiled=True)  82.9 us
    all_gather x1, waiting for transfers between devices, gather_params(): lax.all_gather(part_up, 'fsdp', axis=0, tiled=True)  81.4 us
  transfers between devices with their start and end apart: 20, of which 17 were waited for; matrix products, arithmetic and copies ran while one was open for 11% of the time, Pallas kernels for 0%

commit v1 on v0

--- a/solution.py
+++ b/solution.py
@@ -275,7 +275,7 @@
     local_sq = jnp.zeros((), jnp.float32)
     for grad in reduced:
         local_sq = local_sq + jnp.sum(grad * grad)
-    grad_norm = jnp.sqrt(lax.psum(local_sq, ("dp", "fsdp")))
+    grad_norm = jnp.sqrt(lax.psum(lax.psum(local_sq, "fsdp"), "dp"))
     factor = jnp.minimum(1.0, clip_limit / (grad_norm + 1e-06))
     masters = (w_qkv, w_out, w_up, w_down, time_table, gains)
     firsts = (m_qkv, m_out, m_up, m_down, m_time, m_gains)

time: 1900 us -> 1880 us (0.989)
    psum x1 -> x2, blocking collectives: 40.5 us -> 27.2 us  [on_device(): grad_norm = jnp.sqrt(lax.psum(lax.psum(local_sq, 'fsdp'), 'dp'))]
where the time goes in v1:
time: 1880 us
  waiting for transfers between devices  1420 us (76%)
  matrix products  203 us (11%)
  other arithmetic  91.2 us (5%)
  blocking collectives  81.6 us (4%)
  local copies, waits for them, and re-layouts  62.6 us (3%)
  between operations  22 us (1%)
    unnamed x26, waiting for transfers between devices  392 us
    reduce_scatter x1, waiting for transfers between devices, reduce_grads(): lax.psum_scatter(grad_down.astype(jnp.bfloat16), 'dp', scatter_dimension=...  142 us
    reduce_scatter x1, waiting for transfers between devices, reduce_grads(): lax.psum_scatter(grad_up.astype(jnp.bfloat16), 'dp', scatter_dimension=0,...  127 us
    all_gather x1, waiting for transfers between devices, gather_params(): lax.all_gather(inner_part[3], 'dp', axis=0, tiled=True)  110 us
    reduce_scatter x1, waiting for transfers between devices, reduce_grads(): lax.psum_scatter(outer_part[3].astype(jnp.bfloat16), 'fsdp', scatter_dime...  96.4 us
    reduce_scatter x1, waiting for transfers between devices, reduce_grads(): lax.psum_scatter(outer_part[2].astype(jnp.bfloat16), 'fsdp', scatter_dime...  95 us
    all_gather x1, waiting for transfers between devices, gather_params(): lax.all_gather(inner_part[2], 'dp', axis=0, tiled=True)  82.9 us
    all_gather x1, waiting for transfers between devices, gather_params(): lax.all_gather(part_up, 'fsdp', axis=0, tiled=True)  81.4 us
  transfers between devices with their start and end apart: 20, of which 17 were waited for; matrix products, arithmetic and copies ran while one was open for 11% of the time, Pallas kernels for 0%

profile of v1, /device:TPU:0, one launch (start us, length us, event | category | flops | bytes accessed | tf_op | source)
XLA Modules:
  0.0 1877.8 jit_solution(1437584224939796976)
XLA Ops:
  7.2 2.1 convert_element_type.180
  11.1 2.1 convert_element_type.189
  14.3 64.4 %all-gather.11.cloned.1.call-done = bf16[384,3,1536]{2,0,1:T(8,128)(2,1)} async-done(((bf16[48,3,1536]{2,0,1:T(8,128)(2,1)}), bf16[384,3,1536]{2,0,1:T(8,128)(2,1)}) %all-gather.11.cloned.1.call-update) | async-done | bytes 3538960 | tf_op jit(solution)/shard_map/all_gather | solution.py:49
  78.7 6.0 copy.105
  84.8 36.3 %all-gather.15.cloned.1.call-done = bf16[384,1536]{1,0:T(8,128)(2,1)} async-done(((bf16[48,1536]{1,0:T(8,128)(2,1)}), bf16[384,1536]{1,0:T(8,128)(2,1)}) %all-gather.15.cloned.1.call-update) | async-done | bytes 1179664 | tf_op jit(solution)/shard_map/all_gather | solution.py:50
  121.1 81.4 %all-gather.19.cloned.1.call-done = bf16[384,6144]{1,0:T(8,128)(2,1)} async-done(((bf16[48,6144]{1,0:T(8,128)(2,1)}), bf16[384,6144]{1,0:T(8,128)(2,1)}) %all-gather.19.cloned.1.call-update) | async-done | bytes 4718608 | tf_op jit(solution)/shard_map/all_gather | solution.py:51
  202.6 80.6 %all-gather.23.cloned.1.call-done = bf16[1536,1536]{1,0:T(8,128)(2,1)} async-done(((bf16[192,1536]{1,0:T(8,128)(2,1)}), bf16[1536,1536]{1,0:T(8,128)(2,1)}) %all-gather.23.cloned.1.call-update) | async-done | bytes 4718608 | tf_op jit(solution)/shard_map/all_gather | solution.py:52
  285.2 17.7 all-gather.1
  303.4 5.2 all_gather.47
  308.6 26.0 %all-gather = bf16[8,48,8]{1,2,0:T(8,128)(2,1)S(1)} all-gather(bf16[1,48,8]{1,2,0:T(8,128)(2,1)S(1)} %convert_bitcast_fusion), channel_id=1, replica_groups=mesh['dp'=4,'fsdp'=8] {'fsdp'}, dimensions={0}, use_global_device_ids=true | all-gather | bytes 6912 | tf_op jit(solution)/shard_map/all_gather | solution.py:53
  334.7 5.5 all_gather.45
  345.3 2.5 multiply_convert_fusion.3
  347.8 25.9 %all-gather.13.cloned.1.call-done = bf16[1536,3,1536]{0,2,1:T(8,128)(2,1)} async-done(((bf16[384,3,1536]{0,2,1:T(8,128)(2,1)}), bf16[1536,3,1536]{0,2,1:T(8,128)(2,1)}) %all-gather.13.cloned.1.call-update) | async-done | bytes 14155792 | tf_op jit(solution)/shard_map/all_gather | solution.py:57
  373.8 4.8 fusion.22
  378.6 2.3 copy.107
  380.8 14.0 convolution_convert_fusion.3
  394.8 3.4 fusion.87
  398.2 4.3 copy.108
  402.5 6.1 copy.106
  408.6 10.7 fusion.88
  419.9 12.1 exponential_reduce_fusion
  432.8 11.6 fusion.31
  444.4 4.4 fusion.89
  451.4 82.9 %all-gather.21.cloned.1.call-done = bf16[1536,6144]{1,0:T(8,128)(2,1)} async-done(((bf16[384,6144]{1,0:T(8,128)(2,1)}), bf16[1536,6144]{1,0:T(8,128)(2,1)}) %all-gather.21.cloned.1.call-update) | async-done | bytes 18874384 | tf_op jit(solution)/shard_map/all_gather | solution.py:59
  534.3 11.4 fusion.72
  545.7 110.2 %all-gather.25.cloned.1.call-done = bf16[6144,1536]{1,0:T(8,128)(2,1)} async-done(((bf16[1536,1536]{1,0:T(8,128)(2,1)}), bf16[6144,1536]{1,0:T(8,128)(2,1)}) %all-gather.25.cloned.1.call-update) | async-done | bytes 18874384 | tf_op jit(solution)/shard_map/all_gather | solution.py:60
  655.9 23.5 %add_convert_fusion = (bf16[256,6144]{1,0:T(8,128)(2,1)}, f32[256,6144]{1,0:T(8,128)}) fusion(f32[256,6144]{1,0:T(8,128)} %fusion.72, bf16[256,1536]{1,0:T(8,128)(2,1)} %bitcast.108, bf16[6144,1536]{1,0:T(8,128)(2,1)} %all-gather.25.cloned.1.call-done), kind=kOutput, calls=%fused_computation.22 | convolution fusion | flops 4945084416 | bytes 35389440 | tf_op jit(solution)/shard_map/qd,fd->qf/dot_general | solution.py:213
  679.5 11.8 multiply_reduce_fusion.4
  695.7 2.3 convolution_convert_fusion.7
  698.0 2.3 copy.109
  700.3 11.2 convolution_convert_fusion.6
  711.5 13.3 multiply_reduce_fusion
  724.9 12.7 multiply_convert_fusion
  739.3 4.6 multiply_convert_fusion.1
  743.9 15.7 fusion.2
  760.9 4.1 multiply_reduce_fusion.6
  769.2 3.0 multiply_reduce_fusion.1
  774.9 3.6 convolution_convert_fusion.5
  779.6 3.6 convolution_convert_fusion.4
  783.2 6.8 copy.110
  789.9 18.2 convolution_convert_fusion.2
  808.2 12.5 pad_maximum_fusion
  822.1 12.3 convolution_convert_fusion.1
  834.7 5.7 multiply_convert_fusion.2
  842.0 9.1 convolution_convert_fusion
  852.4 16.1 reduce-scatter.22.cloned.1.call-done
  868.6 112.1 %reduce-scatter.34.cloned.1.call-done = bf16[384,4608]{1,0:T(8,128)(2,1)} async-done(((bf16[1536,4608]{1,0:T(8,128)(2,1)}), bf16[384,4608]{1,0:T(8,128)(2,1)}) %reduce-scatter.34.cloned.1.call-update) | async-done | bytes 3538960
  980.7 5.7 copy.125
  986.4 9.0 copy.112
  995.5 127.5 %reduce-scatter.26.cloned.1.call-done = bf16[384,6144]{1,0:T(8,128)(2,1)} async-done(((bf16[1536,6144]{1,0:T(8,128)(2,1)}), bf16[384,6144]{1,0:T(8,128)(2,1)}) %reduce-scatter.26.cloned.1.call-update) | async-done | bytes 4718608 | tf_op jit(solution)/shard_map/reduce_scatter | solution.py:74
  1123.0 141.9 %reduce-scatter.30.cloned.1.call-done = bf16[1536,1536]{1,0:T(8,128)(2,1)} async-done(((bf16[6144,1536]{1,0:T(8,128)(2,1)}), bf16[1536,1536]{1,0:T(8,128)(2,1)}) %reduce-scatter.30.cloned.1.call-update) | async-done | bytes 4718608 | tf_op jit(solution)/shard_map/reduce_scatter | solution.py:77
  1266.2 10.6 fusion.21
  1276.8 49.2 %reduce-scatter.42.cloned.1.call-done = bf16[48,3]{1,0:T(8,128)(2,1)} async-done(((bf16[384,3]{1,0:T(8,128)(2,1)}), bf16[48,3]{1,0:T(8,128)(2,1)}) %reduce-scatter.42.cloned.1.call-update) | async-done | bytes 304
  1327.5 58.8 %reduce-scatter.38.cloned.1.call-done = bf16[48,8]{1,0:T(8,128)(2,1)} async-done(((bf16[384,8]{1,0:T(8,128)(2,1)}), bf16[48,8]{1,0:T(8,128)(2,1)}) %reduce-scatter.38.cloned.1.call-update) | async-done | bytes 784
  1387.6 65.3 %reduce-scatter.24.cloned.1.call-done = bf16[48,1536]{1,0:T(8,128)(2,1)} async-done(((bf16[384,1536]{1,0:T(8,128)(2,1)}), bf16[48,1536]{1,0:T(8,128)(2,1)}) %reduce-scatter.24.cloned.1.call-update) | async-done | bytes 147472 | tf_op jit(solution)/shard_map/reduce_scatter | solution.py:91
  1454.5 171.0 %all-reduce.3.cloned.1.call-done = bf16[384,3,1536]{2,1,0:T(4,128)(2,1)} async-done(((bf16[384,3,1536]{2,1,0:T(4,128)(2,1)}), bf16[384,3,1536]{2,1,0:T(4,128)(2,1)}) %all-reduce.3.cloned.1.call-update) | async-done | bytes 3538960
  1628.9 95.0 %reduce-scatter.28.cloned.1.call-done = bf16[48,6144]{1,0:T(8,128)(2,1)} async-done(((bf16[384,6144]{1,0:T(8,128)(2,1)}), bf16[48,6144]{1,0:T(8,128)(2,1)}) %reduce-scatter.28.cloned.1.call-update) | async-done | bytes 589840 | tf_op jit(solution)/shard_map/reduce_scatter | solution.py:94
  1726.5 96.4 %reduce-scatter.32.cloned.1.call-done = bf16[192,1536]{1,0:T(8,128)(2,1)} async-done(((bf16[1536,1536]{1,0:T(8,128)(2,1)}), bf16[192,1536]{1,0:T(8,128)(2,1)}) %reduce-scatter.32.cloned.1.call-update) | async-done | bytes 589840 | tf_op jit(solution)/shard_map/reduce_scatter | solution.py:97
  1826.8 20.7 %psum.14 = f32[]{:T(128)} all-reduce(f32[]{:T(128)S(6)} %add.226), channel_id=1, replica_groups=mesh['dp'=4,'fsdp'=8] {'fsdp'}, use_global_device_ids=true, to_apply=%region_40.41 | all-reduce | flops 1 | bytes 8 | tf_op jit(solution)/shard_map/psum | solution.py:278
  1847.5 3.8 add_add_fusion.3
  1851.3 6.6 psum.15
  1859.9 3.7 multiply_subtract_fusion.2
  1864.7 2.4 multiply_subtract_fusion
  1867.2 2.4 multiply_subtract_fusion.1
  (288 shorter events, 47.6 us)
Async XLA Ops:
  7.2 6.1 copy-start.19
  7.2 71.5 %all-gather.11.cloned.1.call-start = ((), (), s32[]{:S(2)}) async-start(), calls=%async_computation.11 | async-start | bytes 3981312 | tf_op jit(solution)/shard_map/all_gather | solution.py:49
  9.3 111.7 %all-gather.15.cloned.1.call-start = ((), (), s32[]{:S(2)}) async-start(), calls=%async_computation.13 | async-start | bytes 1327104 | tf_op jit(solution)/shard_map/all_gather | solution.py:50
  11.1 191.4 %all-gather.19.cloned.1.call-start = ((), (), s32[]{:S(2)}) async-start(), calls=%async_computation.15 | async-start | bytes 5308416 | tf_op jit(solution)/shard_map/all_gather | solution.py:51
  13.3 269.9 %all-gather.23.cloned.1.call-start = ((), (), s32[]{:S(2)}) async-start(), calls=%async_computation.17 | async-start | bytes 5308416 | tf_op jit(solution)/shard_map/all_gather | solution.py:52
  14.2 359.5 %all-gather.13.cloned.1.call-start = ((), (), s32[]{:S(2)}) async-start(), calls=%async_computation.12 | async-start | bytes 17694720 | tf_op jit(solution)/shard_map/all_gather | solution.py:57
  84.8 359.7 %all-gather.17.cloned.1.call-start = ((), (), s32[]{:S(2)}) async-start(), calls=%async_computation.14 | async-start | bytes 5898240 | tf_op jit(solution)/shard_map/all_gather | solution.py:58
  121.1 413.2 %all-gather.21.cloned.1.call-start = ((), (), s32[]{:S(2)}) async-start(), calls=%async_computation.16 | async-start | bytes 23592960 | tf_op jit(solution)/shard_map/all_gather | solution.py:59
  202.5 80.7 %copy-start.2 = (bf16[4,64,1536]{2,1,0:T(8,128)(2,1)S(1)}, bf16[4,64,1536]{2,1,0:T(8,128)(2,1)}, u32[]{:S(2)}) copy-start(bf16[4,64,1536]{2,1,0:T(8,128)(2,1)} %param.22) | copy-start | bytes 2359300
  202.5 82.1 %copy-start.71 = (f32[48,3]{0,1:T(4,128)S(1)}, f32[48,3]{0,1:T(4,128)}, u32[]{:S(2)}) copy-start(f32[48,3]{0,1:T(4,128)} %param.41) | copy-start | bytes 1732
  202.5 100.5 %copy-start.82 = (s32[4]{0:T(128)S(1)}, s32[4]{0:T(128)}, u32[]{:S(2)}) copy-start(s32[4]{0:T(128)} %param.24) | copy-start | bytes 52
  202.5 106.1 %copy-start.62 = (f32[48,8]{0,1:T(8,128)S(1)}, f32[48,8]{0,1:T(8,128)}, u32[]{:S(2)}) copy-start(f32[48,8]{0,1:T(8,128)} %param.38) | copy-start | bytes 4612
  202.5 139.0 %copy-start = (bf16[18,48,1536]{2,1,0:T(8,128)(2,1)S(1)}, bf16[18,48,1536]{2,1,0:T(8,128)(2,1)}, u32[]{:S(2)}) copy-start(bf16[18,48,1536]{2,1,0:T(8,128)(2,1)} %param.23) | copy-start | bytes 7962628
  202.5 453.4 %all-gather.25.cloned.1.call-start = ((), (), s32[]{:S(2)}) async-start(), calls=%async_computation.18 | async-start | bytes 23592960 | tf_op jit(solution)/shard_map/all_gather | solution.py:60
  283.2 568.1 %reduce-scatter.40.cloned.1.call-start = ((), (), s32[]{:S(2)}) async-start(), calls=%async_computation.28 | async-start | bytes 491520
  283.4 19.7 %copy-start.54 = (f32[4,64]{1,0:T(4,128)}, f32[4,64]{1,0:T(4,128)S(1)}, u32[]{:S(2)}) copy-start(f32[4,64]{1,0:T(4,128)S(1)} %broadcast_multiply_fusion.1) | copy-start | bytes 3076
  283.5 64.3 %copy-start.58 = (f32[256]{0:T(256)}, f32[256]{0:T(256)S(1)}, u32[]{:S(2)}) copy-start(f32[256]{0:T(256)S(1)} %div.162) | copy-start | bytes 3076
  284.6 63.3 %copy-start.60 = (f32[256]{0:T(256)}, f32[256]{0:T(256)S(1)}, u32[]{:S(2)}) copy-start(f32[256]{0:T(256)S(1)} %rsqrt.34) | copy-start | bytes 3076
  345.3 28.5 %copy-start.34 = (bf16[256,1536]{1,0:T(8,128)(2,1)S(1)}, bf16[256,1536]{1,0:T(8,128)(2,1)}, u32[]{:S(2)}) copy-start(bf16[256,1536]{1,0:T(8,128)(2,1)} %multiply_convert_fusion.7) | copy-start | bytes 2359300
  373.8 7.1 copy-start.25
  655.9 23.5 %copy-start.5 = (f32[256,1536]{1,0:T(8,128)S(1)}, f32[256,1536]{1,0:T(8,128)}, u32[]{:S(2)}) copy-start(f32[256,1536]{1,0:T(8,128)} %copy-done.4) | copy-start | bytes 4718596
  655.9 23.5 %copy-start.42 = (f32[1536]{0:T(1024)S(1)}, f32[1536]{0:T(1024)}, u32[]{:S(2)}) copy-start(f32[1536]{0:T(1024)} %get-tuple-element.90) | copy-start | bytes 18436
  655.9 23.5 %copy-start.52 = (f32[256]{0:T(256)S(1)}, f32[256]{0:T(256)}, u32[]{:S(2)}) copy-start(f32[256]{0:T(256)} %copy-done.51) | copy-start | bytes 3076
  655.9 23.5 %copy-start.56 = (f32[256]{0:T(256)S(1)}, f32[256]{0:T(256)}, u32[]{:S(2)}) copy-start(f32[256]{0:T(256)} %fusion.66) | copy-start | bytes 3076
  679.4 16.2 slice-start
  679.4 11.9 copy-start.67
  679.5 16.2 slice-start.1
  700.3 11.2 copy-start.16
  739.3 20.8 %copy-start.10 = (bf16[16,96,256]{2,1,0:T(8,128)(2,1)}, bf16[16,96,256]{2,1,0:T(8,128)(2,1)S(1)}, u32[]{:S(2)}) copy-start(bf16[16,96,256]{2,1,0:T(8,128)(2,1)S(1)} %multiply_convert_fusion.5) | copy-start | bytes 2359300
  760.8 5.0 copy-start.1
  760.8 5.0 copy-start.13
  760.8 5.0 copy-start.37
  760.9 5.0 copy-start.45
  769.2 5.6 copy-start.8
  769.2 5.7 copy-start.24
  773.3 78.5 %reduce-scatter.36.cloned.1.call-start = ((), (), s32[]{:S(2)}) async-start(), calls=%async_computation.26 | async-start | bytes 491520
  774.8 93.7 %reduce-scatter.22.cloned.1.call-start = ((), (), s32[]{:S(2)}) async-start(), calls=%async_computation.19 | async-start | bytes 5898240 | tf_op jit(solution)/shard_map/reduce_scatter | solution.py:71
  778.5 202.2 %reduce-scatter.34.cloned.1.call-start = ((), (), s32[]{:S(2)}) async-start(), calls=%async_computation.25 | async-start | bytes 17694720
  783.2 6.8 copy-start.26
  820.7 302.2 %reduce-scatter.26.cloned.1.call-start = ((), (), s32[]{:S(2)}) async-start(), calls=%async_computation.21 | async-start | bytes 23592960 | tf_op jit(solution)/shard_map/reduce_scatter | solution.py:74
  834.4 430.5 %reduce-scatter.30.cloned.1.call-start = ((), (), s32[]{:S(2)}) async-start(), calls=%async_computation.23 | async-start | bytes 23592960 | tf_op jit(solution)/shard_map/reduce_scatter | solution.py:77
  834.6 7.4 copy-start.15
  851.2 474.9 %reduce-scatter.42.cloned.1.call-start = ((), (), s32[]{:S(2)}) async-start(), calls=%async_computation.29 | async-start | bytes 110592
  851.8 534.4 %reduce-scatter.38.cloned.1.call-start = ((), (), s32[]{:S(2)}) async-start(), calls=%async_computation.27 | async-start | bytes 110592
  852.4 600.6 %reduce-scatter.24.cloned.1.call-start = ((), (), s32[]{:S(2)}) async-start(), calls=%async_computation.20 | async-start | bytes 1327104 | tf_op jit(solution)/shard_map/reduce_scatter | solution.py:91
  868.5 757.0 %all-reduce.3.cloned.1.call-start = ((), (), s32[]{:S(2)}) async-start(), calls=%async_computation.30 | async-start | bytes 9437184
  995.5 728.4 %reduce-scatter.28.cloned.1.call-start = ((), (), s32[]{:S(2)}) async-start(), calls=%async_computation.22 | async-start | bytes 5308416 | tf_op jit(solution)/shard_map/reduce_scatter | solution.py:94
  1123.0 142.0 %copy-start.83 = (u32[32]{0:T(128)S(1)}, u32[32]{0:T(128)}, u32[]{:S(2)}) copy-start(u32[32]{0:T(128)} %constant.211) | copy-start | bytes 388
  1123.0 699.9 %reduce-scatter.32.cloned.1.call-start = ((), (), s32[]{:S(2)}) async-start(), calls=%async_computation.24 | async-start | bytes 5308416 | tf_op jit(solution)/shard_map/reduce_scatter | solution.py:97
  1266.2 581.3 %copy-start.65 = (f32[256]{0:T(256)S(1)}, f32[256]{0:T(256)}, u32[]{:S(2)}) copy-start(f32[256]{0:T(256)} %copy-done.64) | copy-start | bytes 3076
  1387.0 471.6 %copy-start.72 = (f32[48,3]{0,1:T(4,128)S(1)}, f32[48,3]{0,1:T(4,128)}, u32[]{:S(2)}) copy-start(f32[48,3]{0,1:T(4,128)} %param.41) | copy-start | bytes 1732
  1387.0 471.6 %copy-start.76 = (f32[48,3]{0,1:T(4,128)S(1)}, f32[48,3]{0,1:T(4,128)}, u32[]{:S(2)}) copy-start(f32[48,3]{0,1:T(4,128)} %param.42) | copy-start | bytes 1732
  1387.0 471.6 %copy-start.77 = (f32[48,3]{0,1:T(4,128)S(1)}, f32[48,3]{0,1:T(4,128)}, u32[]{:S(2)}) copy-start(f32[48,3]{0,1:T(4,128)} %param.43) | copy-start | bytes 1732
  1387.6 471.6 %copy-start.63 = (f32[48,8]{0,1:T(8,128)S(1)}, f32[48,8]{0,1:T(8,128)}, u32[]{:S(2)}) copy-start(f32[48,8]{0,1:T(8,128)} %param.38) | copy-start | bytes 4612
  1387.6 471.6 %copy-start.74 = (f32[48,8]{0,1:T(8,128)S(1)}, f32[48,8]{0,1:T(8,128)}, u32[]{:S(2)}) copy-start(f32[48,8]{0,1:T(8,128)} %param.39) | copy-start | bytes 4612
  1387.6 471.6 %copy-start.75 = (f32[48,8]{0,1:T(8,128)S(1)}, f32[48,8]{0,1:T(8,128)}, u32[]{:S(2)}) copy-start(f32[48,8]{0,1:T(8,128)} %param.40) | copy-start | bytes 4612
  1847.5 16.1 copy-start.29
  1851.2 12.3 copy-start.35
  1851.3 12.3 copy-start.38
  1851.3 12.3 copy-start.39
  1851.3 13.4 copy-start.20
  1851.3 13.4 copy-start.28
  1858.6 6.1 copy-start.30
  1858.6 6.1 copy-start.31
  (42 other events, 99.9 us)
Sparse Core Ops, SparseCore 0:
  10.8 67.8 all-gather.10
  81.5 39.5 all-gather.14
  123.8 78.6 all-gather.18
  205.1 78.0 all-gather.22
  284.6 89.1 all-gather.12
  375.2 37.4 all-gather.16
  414.3 120.0 all-gather.20
  535.9 120.0 all-gather.24
  773.4 20.8 reduce-scatter.39
  797.2 20.7 reduce-scatter.35
  820.6 47.8 reduce-scatter.21
  871.1 109.4 reduce-scatter.33
  983.4 139.4 reduce-scatter.25
  1125.4 139.4 reduce-scatter.29
  1268.4 57.6 reduce-scatter.41
  1329.5 56.6 reduce-scatter.37
  1389.8 63.0 reduce-scatter.23
  1456.8 168.6 all-reduce.2
  1629.6 94.2 reduce-scatter.27
  1727.8 95.0 reduce-scatter.31
